TPU v7x, 256 devices: a whole 4x4x8 slice. The times are simulated.
256 devices in a mesh: gz: 32 (over y, z), gy: 8 (over x, core).
Axes of the slice: x: 4, y: 4, z: 8, core: 2. Of those that a mesh axis runs over, the one named last changes fastest.
Arguments:
- fraction: float32 [256, 256, 512], P('gz', 'gy'), may hold values from 0 to 1
- source: float32 [256, 256, 512], P('gz', 'gy'), may hold values from -40 to 40, as said below
- bubble_label: int32 [256, 256, 512], P('gz', 'gy'), may hold values from -1 to 4095, as said below
- subdomain: int32 [256, 256, 512], P('gz', 'gy'), may hold values from 0 to 1023, as said below
- coarse_inverse: float32 [5120, 5120], P(('gz', 'gy')), may hold values from -0.2 to 0.2, as said below
Outputs:
- iterate: float32 [256, 256, 512], P('gz', 'gy')
- residual: float32 [256, 256, 512], P('gz', 'gy')
Inputs may be any that keep to these rules, and one draw needn't show every extreme that they name: `source`: vertical factor 1 + 2 z / 256, so magnitudes grow with depth. `bubble_label`: A cell at plane z and row y carries -1 or the number of a bubble of slab block a and row block y // 32 with |a - z // 8| <= 1; the bubbles of slab block a and row block b are numbered (a 8 + b) * 16 + i with i < 16. Rows y with y % 32 == 0 carry -1. `subdomain`: cells of slab block a and row block b carry (a 8 + b) * 4 + i with i < 4; the number does not change along z and y inside a block and never falls along x. `coarse_inverse`: symmetric positive definite.
All inputs are finite; a program needn't handle non-finite values.
Results may differ from a plain program's by a relative error of at most 0.0003.
Values sent between devices are 32-bit elements; how exact they have to be, the bound alone decides.
A program may use at most 64 MiB of HBM per device.

v0:
```python
from functools import reduce

import jax
import jax.numpy as jnp
from jax import lax
from jax.sharding import PartitionSpec as P

S_DEV = 4
B_DEV = 16
ITERS = 3


surface_tension = 0.5
shift_term = 0.05
gas_drop = 0.75
norm_floor = 0.25
highest = lax.Precision.HIGHEST


def with_halo(block, sides, width):
    for axis, dim in sides:
        count = lax.axis_size(axis)
        forward = [(i, i + 1) for i in range(count - 1)]
        backward = [(target, source) for source, target in forward]
        low = lax.ppermute(
            lax.slice_in_dim(block, block.shape[dim] - width, None, axis=dim), axis, forward
        )
        high = lax.ppermute(lax.slice_in_dim(block, 0, width, axis=dim), axis, backward)
        block = jnp.concatenate([low, block, high], axis=dim)
    return block


def add_all(items):
    return reduce(lambda first, second: first + second, items)


def widen_x(block):
    return jnp.pad(block, [(0, 0)] * (block.ndim - 1) + [(1, 1)])


def six_neighbours(padded):
    return [
        padded[2:, 1:-1, 1:-1],
        padded[:-2, 1:-1, 1:-1],
        padded[1:-1, 2:, 1:-1],
        padded[1:-1, :-2, 1:-1],
        padded[1:-1, 1:-1, 2:],
        padded[1:-1, 1:-1, :-2],
    ]


def normals(padded):
    along = [
        0.5 * (padded[2:, 1:-1, 1:-1] - padded[:-2, 1:-1, 1:-1]),
        0.5 * (padded[1:-1, 2:, 1:-1] - padded[1:-1, :-2, 1:-1]),
        0.5 * (padded[1:-1, 1:-1, 2:] - padded[1:-1, 1:-1, :-2]),
    ]
    length = jnp.maximum(
        jnp.sqrt(along[0] * along[0] + along[1] * along[1] + along[2] * along[2]), norm_floor
    )
    return jnp.stack([member / length for member in along])


def curvature(padded):
    return -(
        0.5 * (padded[0, 2:, 1:-1, 1:-1] - padded[0, :-2, 1:-1, 1:-1])
        + 0.5 * (padded[1, 1:-1, 2:, 1:-1] - padded[1, 1:-1, :-2, 1:-1])
        + 0.5 * (padded[2, 1:-1, 1:-1, 2:] - padded[2, 1:-1, 1:-1, :-2])
    )


def assemble(frac_padded, kappa_padded, source):
    density = 1.0 - gas_drop * frac_padded
    centre = density[1:-1, 1:-1, 1:-1]
    coefs = [2.0 / (centre + other) for other in six_neighbours(density)]
    fraction = frac_padded[1:-1, 1:-1, 1:-1]
    kappa = kappa_padded[1:-1, 1:-1, 1:-1]
    terms = [
        coef * (0.5 * (kappa + kappa_other)) * (frac_other - fraction)
        for coef, frac_other, kappa_other in zip(
            coefs, six_neighbours(frac_padded), six_neighbours(kappa_padded)
        )
    ]
    rhs = source - surface_tension * add_all(terms)
    diagonal = shift_term + add_all(coefs)
    return (coefs, diagonal, rhs)


def operate_padded(padded, coefs, diagonal):
    return diagonal * padded[1:-1, 1:-1, 1:-1] - add_all(
        [coef * other for coef, other in zip(coefs, six_neighbours(padded))]
    )


def factor_planes(diagonal_planes, down_planes):
    inverse = [1.0 / diagonal_planes[0]]
    mults = [None]
    for level in range(1, len(diagonal_planes)):
        mult = down_planes[level] * inverse[level - 1]
        inverse.append(1.0 / (diagonal_planes[level] - mult * down_planes[level]))
        mults.append(mult)
    return (inverse, mults)


def solve_planes(values, inverse, mults, up_planes):
    count = len(values)
    forward = [values[0]]
    for level in range(1, count):
        forward.append(values[level] + mults[level] * forward[level - 1])
    result = [forward[count - 1] * inverse[count - 1]]
    for level in range(count - 2, -1, -1):
        result.insert(0, (forward[level] + up_planes[level] * result[0]) * inverse[level])
    return result


def region_sums(field, flat_bins, slots):
    flat_field = field.reshape(field.shape[0], -1)

    def one_plane(pair):
        plane_bins, plane_values = pair
        onehot = (plane_bins[None, :] == slots[:, None]).astype(jnp.float32)
        return jnp.dot(onehot, plane_values, precision=highest)

    return jnp.sum(lax.map(one_plane, (flat_bins, flat_field)), axis=0)


def region_values(window, flat_bins, slots):

    def one_plane(plane_bins):
        onehot = (plane_bins[None, :] == slots[:, None]).astype(jnp.float32)
        return jnp.dot(window, onehot, precision=highest)

    return lax.map(one_plane, flat_bins)


def on_device(fraction, source, bubble_label, subdomain, coarse_inverse):
    planes = fraction.shape[0]
    slabs = lax.axis_size("gz")
    columns = lax.axis_size("gy")
    slab_index = lax.axis_index("gz")
    column_index = lax.axis_index("gy")
    devices = slabs * columns
    here = slab_index * columns + column_index
    frac_padded = widen_x(with_halo(fraction, (("gz", 0), ("gy", 1)), 1))
    normal = normals(frac_padded)
    normal_padded = widen_x(with_halo(normal, (("gz", 1), ("gy", 2)), 1))
    kappa = curvature(normal_padded)
    kappa_padded = widen_x(with_halo(kappa, (("gz", 0), ("gy", 1)), 1))
    coefs, diagonal, rhs = assemble(frac_padded, kappa_padded, source)
    inverse, mults = factor_planes(
        [diagonal[level] for level in range(planes)], [coefs[1][level] for level in range(planes)]
    )
    up_planes = [coefs[0][level] for level in range(planes)]
    owner_slab = bubble_label // B_DEV // columns
    bubble_bin = S_DEV + (owner_slab - slab_index + 1) * B_DEV + bubble_label % B_DEV
    bins = jnp.where(bubble_label >= 0, bubble_bin, subdomain - here * S_DEV)
    flat_bins = bins.reshape(planes, -1)
    slots = jnp.arange(S_DEV + 3 * B_DEV, dtype=jnp.int32)
    device_rows = jnp.arange(devices, dtype=jnp.int32)[:, None]
    blank = jnp.zeros((S_DEV,), jnp.float32)

    def precondition(residual):
        block = jnp.stack(
            solve_planes([residual[level] for level in range(planes)], inverse, mults, up_planes)
        )
        partial_value = region_sums(residual, flat_bins, slots)
        own_row = jnp.concatenate(
            [partial_value[:S_DEV], partial_value[S_DEV + B_DEV : S_DEV + 2 * B_DEV]]
        )
        below_row = jnp.concatenate([blank, partial_value[S_DEV : S_DEV + B_DEV]])
        above_row = jnp.concatenate([blank, partial_value[S_DEV + 2 * B_DEV :]])
        spread = (
            jnp.where(device_rows == here, own_row, 0.0)
            + jnp.where(device_rows == here - columns, below_row, 0.0)
            + jnp.where(device_rows == here + columns, above_row, 0.0)
        ).reshape(-1)
        totals = lax.psum(spread, ("gz", "gy"))
        coarse_own = jnp.dot(coarse_inverse, totals, precision=highest)
        bubble_rows = with_halo(coarse_own[S_DEV:][None, :], (("gz", 0),), 1)
        window = jnp.concatenate(
            [coarse_own[:S_DEV], bubble_rows[0], coarse_own[S_DEV:], bubble_rows[2]]
        )
        correction = region_values(window, flat_bins, slots).reshape(residual.shape)
        direction = block + correction
        product = lax.psum(jnp.sum(residual * direction), ("gz", "gy"))
        return (direction, product)

    iterate = jnp.zeros_like(rhs)
    residual = rhs
    direction, product = precondition(residual)
    search = direction
    for sweep in range(ITERS):
        padded = widen_x(with_halo(search, (("gz", 0), ("gy", 1)), 1))
        image = operate_padded(padded, coefs, diagonal)
        alpha = product / lax.psum(jnp.sum(search * image), ("gz", "gy"))
        iterate = iterate + alpha * search
        residual = residual - alpha * image
        if sweep + 1 < ITERS:
            direction, fresh = precondition(residual)
            search = direction + fresh / product * search
            product = fresh
    return (iterate, residual)


def solution(mesh):
    placed = (
        P("gz", "gy", None),
        P("gz", "gy", None),
        P("gz", "gy", None),
        P("gz", "gy", None),
        P(("gz", "gy"), None),
    )
    return jax.shard_map(
        on_device,
        mesh=mesh,
        in_specs=placed,
        out_specs=(P("gz", "gy", None), P("gz", "gy", None)),
        check_vma=False,
    )
```

profile of v0, /device:TPU:1, one launch (start us, length us, event | category | flops | bytes accessed | tf_op | source)
XLA Modules:
  0.0 992.9 jit_solution(13966434582722056104)
XLA Ops:
  1.6 4.4 collective-permute-start
  11.3 4.9 collective-permute-start.2
  25.9 4.2 collective-permute-start.5
  44.5 4.6 select_maximum_fusion
  51.7 5.1 collective-permute-start.9
  66.3 7.0 fusion.75
  74.4 32.1 %while.66 = (s32[]{:T(128)}, f32[8,52]{1,0:T(8,128)S(1)}, s32[8,16384]{1,0:T(8,128)}, f32[8,16384]{1,0:T(8,128)}, s32[]{:T(128)}, /*index=5*/s32[]{:T(128)}) while((s32[]{:T(128)}, f32[8,52]{1,0:T(8,128)S(1)}, s32[8,16384]{1,0:T(8,128)}, f32[8,16384]{1,0:T(8,128)}, s32[]{:T(128)}, /*index=5*/s32[]{:T(128)}) %tuple.202), condition=%wide.region_1.2_spmd.clone, body=%wide.region_0.1_spmd.clone.sunk | while | flops 11075586 | bytes 263357 | solution.py:124
  107.1 85.8 %psum.63 = f32[5120]{0:T(1024)S(1)} all-reduce(f32[5120]{0:T(1024)S(1)} %add.709), channel_id=1, replica_groups=mesh['gz'=32,'gy'=8] {'gz','gy'}, use_global_device_ids=true, to_apply=%region_3.4 | all-reduce | flops 5120 | bytes 40960 | tf_op jit(solution)/shard_map/psum | solution.py:177
  194.8 4.5 collective-permute-start.12
  203.7 23.2 %while.67 = (s32[]{:T(128)}, f32[8,16384]{1,0:T(8,128)S(1)}, s32[8,16384]{1,0:T(8,128)}, f32[52]{0:T(128)S(1)}, s32[]{:T(128)}, /*index=5*/s32[]{:T(128)}) while((s32[]{:T(128)}, f32[8,16384]{1,0:T(8,128)S(1)}, s32[8,16384]{1,0:T(8,128)}, f32[52]{0:T(128)S(1)}, s32[]{:T(128)}, /*index=5*/s32[]{:T(128)}) %tuple.197), condition=%wide.region_5.6_spmd.clone, body=%wide.region_4.5_spmd.clone.sunk | while | flops 11075586 | bytes 393501 | solution.py:133
  235.9 4.0 collective-permute-start.16
  247.4 80.5 %all-reduce.12 = (f32[]{:T(128)}, f32[]{:T(128)}) all-reduce(f32[]{:T(128)} %get-tuple-element.231, f32[]{:T(128)} %get-tuple-element.230), channel_id=1, replica_groups=mesh['gz'=32,'gy'=8] {'gz','gy'}, use_global_device_ids=true, to_apply=%region_7.8 | all-reduce | flops 2 | bytes 16 | tf_op jit(solution)/shard_map/psum | solution.py:185
  333.3 32.1 %while.68 = (s32[]{:T(128)}, f32[8,52]{1,0:T(8,128)S(1)}, s32[8,16384]{1,0:T(8,128)}, f32[8,16384]{1,0:T(8,128)}, s32[]{:T(128)}, /*index=5*/s32[]{:T(128)}) while((s32[]{:T(128)}, f32[8,52]{1,0:T(8,128)S(1)}, s32[8,16384]{1,0:T(8,128)}, f32[8,16384]{1,0:T(8,128)}, s32[]{:T(128)}, /*index=5*/s32[]{:T(128)}) %tuple.203), condition=%wide.region_11.12_spmd.clone, body=%wide.region_10.11_spmd.clone.sunk | while | flops 11075586 | bytes 263357 | solution.py:124
  366.0 73.9 %psum.66 = f32[5120]{0:T(1024)S(1)} all-reduce(f32[5120]{0:T(1024)S(1)} %add.732), channel_id=1, replica_groups=mesh['gz'=32,'gy'=8] {'gz','gy'}, use_global_device_ids=true, to_apply=%region_13.14 | all-reduce | flops 5120 | bytes 40960 | tf_op jit(solution)/shard_map/psum | solution.py:177
  448.7 23.2 %while.69 = (s32[]{:T(128)}, f32[8,16384]{1,0:T(8,128)S(1)}, s32[8,16384]{1,0:T(8,128)}, f32[52]{0:T(128)S(1)}, s32[]{:T(128)}, /*index=5*/s32[]{:T(128)}) while((s32[]{:T(128)}, f32[8,16384]{1,0:T(8,128)S(1)}, s32[8,16384]{1,0:T(8,128)}, f32[52]{0:T(128)S(1)}, s32[]{:T(128)}, /*index=5*/s32[]{:T(128)}) %tuple.199), condition=%wide.region_15.16_spmd.clone, body=%wide.region_14.15_spmd.clone.sunk | while | flops 11075586 | bytes 393501 | solution.py:133
  474.3 76.8 %psum.67 = f32[]{:T(128)} all-reduce(f32[]{:T(128)} %multiply_reduce_fusion.3), channel_id=1, replica_groups=mesh['gz'=32,'gy'=8] {'gz','gy'}, use_global_device_ids=true, to_apply=%region_17.18 | all-reduce | flops 1 | bytes 8 | tf_op jit(solution)/shard_map/psum | solution.py:185
  555.5 4.3 collective-permute-start.21
  573.4 78.3 %psum.68 = f32[]{:T(128)} all-reduce(f32[]{:T(128)} %get-tuple-element.294), channel_id=1, replica_groups=mesh['gz'=32,'gy'=8] {'gz','gy'}, use_global_device_ids=true, to_apply=%region_19.20 | all-reduce | flops 1 | bytes 8 | tf_op jit(solution)/shard_map/psum | solution.py:195
  655.3 32.0 %while.70 = (s32[]{:T(128)}, f32[8,52]{1,0:T(8,128)S(1)}, s32[8,16384]{1,0:T(8,128)}, f32[8,16384]{1,0:T(8,128)}, s32[]{:T(128)}, /*index=5*/s32[]{:T(128)}) while((s32[]{:T(128)}, f32[8,52]{1,0:T(8,128)S(1)}, s32[8,16384]{1,0:T(8,128)}, f32[8,16384]{1,0:T(8,128)}, s32[]{:T(128)}, /*index=5*/s32[]{:T(128)}) %tuple.204), condition=%wide.region_21.22_spmd.clone, body=%wide.region_20.21_spmd.clone.sunk | while | flops 11075586 | bytes 263357 | solution.py:124
  689.5 73.9 %psum.69 = f32[5120]{0:T(1024)S(1)} all-reduce(f32[5120]{0:T(1024)S(1)} %add.757), channel_id=1, replica_groups=mesh['gz'=32,'gy'=8] {'gz','gy'}, use_global_device_ids=true, to_apply=%region_23.24 | all-reduce | flops 5120 | bytes 40960 | tf_op jit(solution)/shard_map/psum | solution.py:177
  776.2 34.6 %while.71 = (s32[]{:T(128)}, f32[8,16384]{1,0:T(8,128)}, s32[8,16384]{1,0:T(8,128)}, f32[52]{0:T(128)S(1)}, s32[]{:T(128)}, /*index=5*/s32[]{:T(128)}) while((s32[]{:T(128)}, f32[8,16384]{1,0:T(8,128)}, s32[8,16384]{1,0:T(8,128)}, f32[52]{0:T(128)S(1)}, s32[]{:T(128)}, /*index=5*/s32[]{:T(128)}) %tuple.201), condition=%wide.region_25.26_spmd.clone, body=%wide.region_24.25_spmd.clone.sunk | while | flops 11075586 | bytes 393501 | solution.py:133
  812.9 76.7 %psum.70 = f32[]{:T(128)} all-reduce(f32[]{:T(128)} %multiply_reduce_fusion.1), channel_id=1, replica_groups=mesh['gz'=32,'gy'=8] {'gz','gy'}, use_global_device_ids=true, to_apply=%region_27.28 | all-reduce | flops 1 | bytes 8 | tf_op jit(solution)/shard_map/psum | solution.py:185
  894.1 4.3 collective-permute-start.27
  909.0 78.3 %psum.71 = f32[]{:T(128)} all-reduce(f32[]{:T(128)} %get-tuple-element.282), channel_id=1, replica_groups=mesh['gz'=32,'gy'=8] {'gz','gy'}, use_global_device_ids=true, to_apply=%region_29.30 | all-reduce | flops 1 | bytes 8 | tf_op jit(solution)/shard_map/psum | solution.py:195
  (382 shorter events, 311.9 us)
Async XLA Ops:
  1.6 5.7 collective-permute-start
  11.3 6.9 collective-permute-start.2
  24.5 7.1 collective-permute-start.4
  25.9 7.4 collective-permute-start.5
  34.6 8.7 collective-permute-start.6
  36.5 6.8 collective-permute-start.7
  50.2 6.5 collective-permute-start.8
  51.7 6.4 collective-permute-start.9
  58.1 7.8 collective-permute-start.10
  60.0 5.8 collective-permute-start.11
  193.5 9.3 collective-permute-start.13
  194.8 8.0 collective-permute-start.12
  229.2 5.3 collective-permute-start.14
  230.5 5.3 collective-permute-start.15
  235.9 6.6 collective-permute-start.16
  440.5 7.4 collective-permute-start.18
  554.2 5.6 collective-permute-start.20
  555.5 5.6 collective-permute-start.21
  561.8 5.8 collective-permute-start.22
  764.0 11.3 %collective-permute-start.24 = (f32[1,16]{1,0:T(1,128)S(1)}, f32[1,16]{1,0:T(1,128)S(1)}, u32[]{:S(2)}, u32[]{:S(2)}) collective-permute-start(f32[1,16]{1,0:T(1,128)S(1)} %get-tuple-element.369), channel_id=1, source_target_pairs={{0,8},{8,16},{16,24},{24,32},{32,40},{40,48},{48,56},{56,64},{64,7... | collective-permute-start | bytes 200 | tf_op jit(solution)/shard_map/ppermute | solution.py:25
  766.8 8.5 collective-permute-start.25
  892.8 5.6 collective-permute-start.26
  894.1 5.6 collective-permute-start.27
  899.7 5.8 collective-permute-start.28
  (46 other events, 2401.1 us)
where the time goes:
time: 1010 us; the launch traced here: 993 us
  blocking collectives  624 us (62%)
  matrix products  101 us (10%)
  local copies, waits for them, and re-layouts  95.5 us (9%)
  starting transfers between devices  84.6 us (8%)
  other arithmetic  60.3 us (6%)
  waiting for transfers between devices  17.2 us (2%)
    psum x3, blocking collectives, precondition(): product = lax.psum(jnp.sum(residual * direction), ('gz', 'gy'))  234 us
    psum x3, blocking collectives, precondition(): totals = lax.psum(spread, ('gz', 'gy'))  234 us
    psum x2, blocking collectives, on_device(): alpha = product / lax.psum(jnp.sum(search * image), ('gz', 'gy'))  157 us
    dot_general x24, matrix products, one_plane(): return jnp.dot(onehot, plane_values, precision=highest)  68.5 us
    ppermute x15, starting transfers between devices, with_halo(): lax.ppermute(lax.slice_in_dim(block, block.shape[dim] - width, None, axis...  56.1 us
    dynamic_slice x48, local copies, waits for them, and re-layouts, region_sums(): return jnp.sum(lax.map(one_plane, (flat_bins, flat_field)), axis=0)  52.5 us
    dot_general x24, matrix products, one_plane(): return jnp.dot(window, onehot, precision=highest)  31.3 us
    ppermute x15, starting transfers between devices, with_halo(): lax.ppermute(lax.slice_in_dim(block, 0, width, axis=dim), axis, backward)  28.5 us
  transfers between devices with their start and end apart: 30, of which 11 were waited for; matrix products, arithmetic and copies ran while one was open for 2% of the time, Pallas kernels for 0%

commit v1 on v0

v1 whole, which is shorter than its diff:
```python
import functools

import jax
import jax.numpy as jnp
from jax import lax
from jax.experimental import pallas as pl
from jax.experimental.pallas import tpu as pltpu
from jax.sharding import PartitionSpec as P

MESH = pl.DeviceIdType.MESH
CZ, CY, NX = 8, 32, 512
S_DEV, B_DEV = 4, 16
SPAN = S_DEV + B_DEV
SLABS, COLS = 32, 8
DEVS = SLABS * COLS
f32 = jnp.float32


def lanes_of(shape):
    return lax.broadcasted_iota(jnp.int32, shape, len(shape) - 1)


def x_plus(v):
    n = v.shape[-1]
    return jnp.where(lanes_of(v.shape) == n - 1, 0.0, pltpu.roll(v, n - 1, 1))


def x_minus(v):
    return jnp.where(lanes_of(v.shape) == 0, 0.0, pltpu.roll(v, 1, 1))


def far_first(n, half):
    return half + ((n + 1) // 2) * (1 - 2 * lax.rem(n, 2))


def kernel(
    frac, src, lab, sub, cinv, out_x, out_r,
    F, NRM, KAP, SRC, LB, SB, BN, CV, CW, CZF, CYP, CYM, CXP, CXM, DG, IV,
    R0, W, BL, Z, HBZ, HBY, HZ, HY, HBN, HYO, T2, X, YB, YS, M, G, M3, G3,
    ld, fs, fr, bsn, brc, cs, cr, ks, kr, gs, gr,
):
    a = lax.axis_index("gz")
    b = lax.axis_index("gy")
    me = b * SLABS + a
    here = a * COLS + b
    phys_y, phys_z, phys_x, core = a // 8, lax.rem(a, 8), b // 2, lax.rem(b, 2)
    up, down = lax.rem(a + 1, SLABS), lax.rem(a + SLABS - 1, SLABS)
    right, left = lax.rem(b + 1, COLS), lax.rem(b + COLS - 1, COLS)

    loads = [
        pltpu.make_async_copy(frac, F.at[pl.ds(3, CZ), pl.ds(16, CY)], ld.at[0]),
        pltpu.make_async_copy(src, SRC, ld.at[1]),
        pltpu.make_async_copy(lab, LB, ld.at[2]),
        pltpu.make_async_copy(sub, SB, ld.at[3]),
        pltpu.make_async_copy(cinv, CV, ld.at[4]),
    ]
    for copy in loads:
        copy.start()

    def partner(k):
        ty = lax.rem(phys_y + far_first(lax.rem(k // 8, 4), 2), 4)
        tz = lax.rem(phys_z + far_first(k // 32, 4), 8)
        tx = lax.rem(phys_x + far_first(lax.rem(k // 2, 4), 2), 4)
        tc = lax.rem(core + 1 - lax.rem(k, 2), 2)
        ta, tb = ty * 8 + tz, tx * 2 + tc
        return ta, tb

    bar = pltpu.get_barrier_semaphore()

    def greet(k, c):
        pl.semaphore_signal(bar, inc=1, device_id=partner(k), device_id_type=MESH)
        return c

    lax.fori_loop(0, DEVS - 1, greet, 0)
    pl.semaphore_wait(bar, DEVS - 1)

    def remote(source, target, send, recv, device):
        return pltpu.make_async_remote_copy(
            src_ref=source, dst_ref=target, send_sem=send, recv_sem=recv, device_id=device, device_id_type=MESH
        )

    halo = [
        remote(frac.at[pl.ds(0, 3)], F.at[pl.ds(11, 3), pl.ds(16, CY)], fs.at[0], fr.at[0], (down, b)),
        remote(frac.at[pl.ds(5, 3)], F.at[pl.ds(0, 3), pl.ds(16, CY)], fs.at[1], fr.at[1], (up, b)),
        remote(frac.at[:, pl.ds(24, 8)], F.at[pl.ds(3, CZ), pl.ds(8, 8)], fs.at[2], fr.at[2], (a, right)),
        remote(frac.at[:, pl.ds(0, 8)], F.at[pl.ds(3, CZ), pl.ds(48, 8)], fs.at[3], fr.at[3], (a, left)),
        remote(frac.at[pl.ds(6, 2), pl.ds(24, 8)], F.at[pl.ds(1, 2), pl.ds(8, 8)], fs.at[4], fr.at[4], (up, right)),
        remote(frac.at[pl.ds(6, 2), pl.ds(0, 8)], F.at[pl.ds(1, 2), pl.ds(48, 8)], fs.at[5], fr.at[5], (up, left)),
        remote(frac.at[pl.ds(0, 2), pl.ds(24, 8)], F.at[pl.ds(11, 2), pl.ds(8, 8)], fs.at[6], fr.at[6], (down, right)),
        remote(frac.at[pl.ds(0, 2), pl.ds(0, 8)], F.at[pl.ds(11, 2), pl.ds(48, 8)], fs.at[7], fr.at[7], (down, left)),
    ]
    for copy in halo:
        copy.start()

    loads[2].wait()
    loads[3].wait()

    def bins_plane(z, c):
        label, domain = LB[z], SB[z]
        off = (label >> 7) - a
        shift = jnp.where(off == 0, S_DEV, jnp.where(off < 0, SPAN, SPAN + B_DEV))
        BN[z] = jnp.where(label >= 0, (label & 15) + shift, domain - here * S_DEV)
        return c

    lax.fori_loop(0, CZ, bins_plane, 0)
    bins_out = [
        remote(BN.at[0], HBZ.at[1], bsn.at[0], brc.at[0], (down, b)),
        remote(BN.at[CZ - 1], HBZ.at[0], bsn.at[1], brc.at[1], (up, b)),
        remote(BN.at[:, pl.ds(24, 8)], HBY.at[0], bsn.at[2], brc.at[2], (a, right)),
        remote(BN.at[:, pl.ds(0, 8)], HBY.at[1], bsn.at[3], brc.at[3], (a, left)),
    ]
    for copy in bins_out:
        copy.start()

    loads[4].wait()
    first = CV[pl.ds(0, 8), :]
    CW[pl.ds(0, 8), :] = jnp.where(lax.broadcasted_iota(jnp.int32, first.shape, 0) < S_DEV, first, 0.0)
    CW[pl.ds(8, B_DEV), :] = CV[pl.ds(S_DEV, B_DEV), :]
    rows_out = [
        remote(CW.at[pl.ds(8, B_DEV)], CW.at[pl.ds(24, B_DEV)], cs.at[0], cr.at[0], (up, b)),
        remote(CW.at[pl.ds(8, B_DEV)], CW.at[pl.ds(40, B_DEV)], cs.at[1], cr.at[1], (down, b)),
    ]
    for copy in rows_out:
        copy.start()
    X[...] = jnp.zeros_like(X)
    YB[...] = jnp.zeros_like(YB)
    YS[...] = jnp.zeros_like(YS)
    T2[...] = jnp.zeros_like(T2)

    loads[0].wait()
    loads[1].wait()
    for copy in halo:
        copy.wait_recv()

    @pl.when(a == 0)
    def _():
        F[pl.ds(0, 3)] = jnp.zeros((3,) + F.shape[1:], f32)

    @pl.when(a == SLABS - 1)
    def _():
        F[pl.ds(11, 3)] = jnp.zeros((3,) + F.shape[1:], f32)

    @pl.when(b == 0)
    def _():
        F[:, pl.ds(8, 8)] = jnp.zeros((F.shape[0], 8, NX), f32)

    @pl.when(b == COLS - 1)
    def _():
        F[:, pl.ds(48, 8)] = jnp.zeros((F.shape[0], 8, NX), f32)

    def row_valid(first_row, shape):
        row = lax.broadcasted_iota(jnp.int32, shape, 0) + (first_row - 16 + b * CY)
        return (row >= 0) & (row < COLS * CY)

    def z_valid(z):
        place = a * CZ + z
        return (place >= 0) & (place < SLABS * CZ)

    wide = (8, 24, 40)

    def normals_plane(n, c):
        inside = z_valid(n - 2)
        for r in wide:
            rows = pl.ds(r, 16)
            centre = F[n + 1, rows, :]
            gz = 0.5 * (F[n + 2, rows, :] - F[n, rows, :])
            gy = 0.5 * (F[n + 1, pl.ds(r + 1, 16), :] - F[n + 1, pl.ds(r - 1, 16), :])
            gx = 0.5 * (x_plus(centre) - x_minus(centre))
            scale = jnp.minimum(lax.rsqrt(gz * gz + gy * gy + gx * gx), 4.0)
            scale = jnp.where(row_valid(r, scale.shape) & inside, scale, 0.0)
            NRM[0, n, rows, :] = gz * scale
            NRM[1, n, rows, :] = gy * scale
            NRM[2, n, rows, :] = gx * scale
        return c

    lax.fori_loop(0, CZ + 4, normals_plane, 0)

    def kappa_plane(n, c):
        inside = z_valid(n - 1)
        for r in wide:
            rows = pl.ds(r, 16)
            nx = NRM[2, n + 1, rows, :]
            value = -(
                0.5 * (NRM[0, n + 2, rows, :] - NRM[0, n, rows, :])
                + 0.5 * (NRM[1, n + 1, pl.ds(r + 1, 16), :] - NRM[1, n + 1, pl.ds(r - 1, 16), :])
                + 0.5 * (x_plus(nx) - x_minus(nx))
            )
            KAP[n, rows, :] = jnp.where(row_valid(r, value.shape) & inside, value, 0.0)
        return c

    lax.fori_loop(0, CZ + 2, kappa_plane, 0)

    def density(v):
        return 1.0 - 0.75 * v

    def faces_plane(n, c):
        for r in (0, 16):
            rows = pl.ds(16 + r, 16)
            CZF[n, pl.ds(r, 16), :] = 2.0 / (density(F[n + 2, rows, :]) + density(F[n + 3, rows, :]))
        return c

    lax.fori_loop(0, CZ + 1, faces_plane, 0)

    def assemble_plane(z, c):
        for r in range(0, CY, 8):
            rows, mine = pl.ds(16 + r, 8), pl.ds(r, 8)
            fc, kc = F[z + 3, rows, :], KAP[z + 1, rows, :]
            dc = density(fc)
            fy = (F[z + 3, pl.ds(17 + r, 8), :], F[z + 3, pl.ds(15 + r, 8), :])
            fx = (x_plus(fc), x_minus(fc))
            cz = (CZF[z + 1, mine, :], CZF[z, mine, :])
            cy = tuple(2.0 / (dc + density(v)) for v in fy)
            cx = tuple(2.0 / (dc + density(v)) for v in fx)
            CYP[z, mine, :], CYM[z, mine, :] = cy
            CXP[z, mine, :], CXM[z, mine, :] = cx
            DG[z, mine, :] = 0.05 + (cz[0] + cz[1] + cy[0] + cy[1] + cx[0] + cx[1])
            term = cz[0] * (0.5 * (kc + KAP[z + 2, rows, :])) * (F[z + 4, rows, :] - fc)
            term = term + cz[1] * (0.5 * (kc + KAP[z, rows, :])) * (F[z + 2, rows, :] - fc)
            term = term + cy[0] * (0.5 * (kc + KAP[z + 1, pl.ds(17 + r, 8), :])) * (fy[0] - fc)
            term = term + cy[1] * (0.5 * (kc + KAP[z + 1, pl.ds(15 + r, 8), :])) * (fy[1] - fc)
            term = term + cx[0] * (0.5 * (kc + x_plus(kc))) * (fx[0] - fc)
            term = term + cx[1] * (0.5 * (kc + x_minus(kc))) * (fx[1] - fc)
            R0[z, mine, :] = SRC[z, mine, :] - 0.5 * term
        return c

    lax.fori_loop(0, CZ, assemble_plane, 0)

    def factor_rows(i, c):
        rows = pl.ds(pl.multiple_of(i * 8, 8), 8)
        inverse = 1.0 / DG[0, rows, :]
        IV[0, rows, :] = inverse
        for z in range(1, CZ):
            face = CZF[z, rows, :]
            inverse = 1.0 / (DG[z, rows, :] - (face * inverse) * face)
            IV[z, rows, :] = inverse
        return c

    lanes_row = lanes_of((1, 128))

    def region_sums(v_ref):
        for group in range(3):
            base = S_DEV + B_DEV * group

            def tile(t, acc, base=base, group=group):
                z, rows = t // 4, pl.ds(pl.multiple_of(lax.rem(t, 4) * 8, 8), 8)
                bins, v = BN[z, rows, :], v_ref[z, rows, :]
                new = []
                for k in range(B_DEV):
                    picked = jnp.where(bins == base + k, v, 0.0)
                    new.append(
                        acc[k]
                        + ((picked[:, 0:128] + picked[:, 128:256]) + (picked[:, 256:384] + picked[:, 384:512]))
                    )
                return tuple(new)

            acc = lax.fori_loop(0, CZ * 4, tile, tuple(jnp.zeros((8, 128), f32) for _ in range(B_DEV)))
            for k in range(B_DEV):
                T2[pl.ds(8 + B_DEV * group + k, 1), :] = jnp.sum(acc[k], axis=0, keepdims=True)

        def liquid(t, acc):
            z, rows = t // 4, pl.ds(pl.multiple_of(lax.rem(t, 4) * 8, 8), 8)
            return acc + jnp.where(BN[z, rows, :] < S_DEV, v_ref[z, rows, :], 0.0)

        acc = lax.fori_loop(0, CZ * 4, liquid, jnp.zeros((8, NX), f32))
        domain = SB[0, pl.ds(0, 8), :] - here * S_DEV
        for k in range(S_DEV):
            picked = jnp.sum(jnp.where(domain == k, acc, 0.0), axis=0, keepdims=True)
            T2[pl.ds(k, 1), :] = (picked[:, 0:128] + picked[:, 128:256]) + (picked[:, 256:384] + picked[:, 384:512])
        return jnp.sum(T2[...], axis=1, keepdims=True)

    def exchange(k, sums, dots):
        for g in range(8):
            part = jnp.sum(CW[:, pl.ds(640 * g, 640)] * sums, axis=0, keepdims=True)
            for j in range(4):
                moved = part if j == 0 else pltpu.roll(part, 640 - 160 * j, 1)
                X[pl.ds(8 + 4 * g + j, 1), :] = moved[:, 0:256]
        wide_lanes = lanes_of((SLABS, 128))
        rows = pl.ds(8, SLABS)
        for t in range(COLS):
            if t <= 5:
                moved = X[rows, pl.ds(0, 128)]
                moved = moved if t == 0 else pltpu.roll(moved, 128 - SPAN * t, 1)
            elif t == 6:
                moved = pltpu.roll(X[rows, :], 256 - SPAN * t, 1)[:, 0:128]
            else:
                moved = pltpu.roll(X[rows, pl.ds(128, 128)], 256 - SPAN * t, 1)
            YS[t, rows, :] = jnp.where(wide_lanes < S_DEV, moved, 0.0)
            YB[t, rows, :] = jnp.where((wide_lanes >= S_DEV) & (wide_lanes < SPAN), moved, 0.0)
        before = None
        for t in range(COLS):
            row0 = (
                (YS[t, rows, :] + YB[t, rows, :])
                + pltpu.roll(YB[t, pl.ds(7, SLABS), :], 16, 1)
                + pltpu.roll(YB[t, pl.ds(9, SLABS), :], 32, 1)
                + pltpu.roll(YB[t, pl.ds(6, SLABS), :], 48, 1)
                + pltpu.roll(YB[t, pl.ds(10, SLABS), :], 64, 1)
                + pltpu.roll(YS[t, pl.ds(7, SLABS), :], 84, 1)
                + pltpu.roll(YS[t, pl.ds(9, SLABS), :], 88, 1)
            )
            if t + 1 < COLS:
                row0 = row0 + pltpu.roll(YS[t + 1, rows, :], 92, 1)
            row1 = jnp.broadcast_to(dots, (SLABS, 128))
            if before is not None:
                row1 = row1 + jnp.where(wide_lanes < SPAN + 2 * B_DEV, before, 0.0)
            M[k, pl.ds(SLABS * t, SLABS), 0, :] = row0
            M[k, pl.ds(SLABS * t, SLABS), 1, :] = row1
            before = row0

        def post(n, c):
            ta, tb = partner(n)
            remote(M.at[k, tb * SLABS + ta], G.at[k, me], gs.at[k], gr.at[k], (ta, tb)).start()
            return c

        lax.fori_loop(0, DEVS - 1, post, 0)
        G[k, me] = M[k, me]

    def collect(k):
        part = G.at[k, pl.ds(0, DEVS - 1)]
        pltpu.make_async_copy(part, part, gr.at[k]).wait()

        def add(i, acc):
            return acc + G[k, pl.ds(8 * i, 8)]

        total = jnp.sum(lax.fori_loop(0, DEVS // 8, add, jnp.zeros((8, 2, 128), f32)), axis=0)
        return total[0:1, :], total[1:2, :]

    def block_solve(v_ref, o_ref):
        def solve_rows(i, c):
            rows = pl.ds(pl.multiple_of(i * 8, 8), 8)
            inv = [IV[z, rows, :] for z in range(CZ)]
            face = [CZF[z, rows, :] for z in range(1, CZ)]
            held = [v_ref[0, rows, :] * inv[0]]
            for z in range(1, CZ):
                held.append((v_ref[z, rows, :] + face[z - 1] * held[z - 1]) * inv[z])
            value = held[CZ - 1]
            o_ref[CZ - 1, rows, :] = value
            for z in range(CZ - 2, -1, -1):
                value = held[z] + (face[z] * value) * inv[z]
                o_ref[z, rows, :] = value
            return c

        lax.fori_loop(0, CY // 8, solve_rows, 0)

    def send_block_halo(k):
        o_ref = BL.at[k]
        for z in range(CZ):
            HYO[k, 0, pl.ds(z, 1), :] = BL[k, z, pl.ds(CY - 1, 1), :]
            HYO[k, 1, pl.ds(z, 1), :] = BL[k, z, pl.ds(0, 1), :]
        out = [
            remote(o_ref.at[0], HZ.at[k, 1], ks.at[k, 0], kr.at[k, 0], (down, b)),
            remote(o_ref.at[CZ - 1], HZ.at[k, 0], ks.at[k, 1], kr.at[k, 1], (up, b)),
            remote(HYO.at[k, 0], HY.at[k, 0], ks.at[k, 2], kr.at[k, 2], (a, right)),
            remote(HYO.at[k, 1], HY.at[k, 1], ks.at[k, 3], kr.at[k, 3], (a, left)),
        ]
        for copy in out:
            copy.start()
        return out

    def pick(table, bins):
        rows = bins.shape[0]
        spread = jnp.broadcast_to(table, (rows, 128))
        return jnp.concatenate(
            [
                jnp.take_along_axis(spread, bins[:, 128 * i : 128 * i + 128], axis=1, mode="promise_in_bounds")
                for i in range(NX // 128)
            ],
            axis=1,
        )

    def combine(ref_at, coefs):
        value = ref_at(0)
        for i, coef in enumerate(coefs):
            value = value - coef * ref_at(i + 1)
        return value

    def total_of(acc):
        part = jnp.sum(acc, axis=0, keepdims=True)
        return jnp.sum(part, axis=1, keepdims=True)

    def direction(k, tables0, tables1, coefs, other):
        table0 = combine(lambda i: tables0[i], coefs)
        table1 = combine(lambda i: tables1[i], coefs)

        def plane(z, acc):
            rz, zs = acc
            for r in range(0, CY, 8):
                rows = pl.ds(r, 8)
                value = combine(lambda i: BL[i, z, rows, :], coefs) + pick(table0, BN[z, rows, :])
                Z[k, z + 1, pl.ds(8 + r, 8), :] = value
                res = R0[z, rows, :]
                for i, coef in enumerate(coefs):
                    res = res - coef * W[i, z, rows, :]
                rz = rz + res * value
                if k > 0:
                    image = W[k - 1, z, rows, :]
                    if k > 1:
                        image = image + other * W[0, z, rows, :]
                    zs = zs + image * value
            return rz, zs

        zero = jnp.zeros((8, NX), f32)
        rz, zs = lax.fori_loop(0, CZ, plane, (zero, zero))
        for side in range(2):
            inside = a > 0 if side == 0 else a < SLABS - 1
            for r in range(0, CY, 8):
                rows = pl.ds(r, 8)
                value = combine(lambda i: HZ[i, side, rows, :], coefs) + pick(table0, HBZ[side, rows, :])
                Z[k, (CZ + 1) * side, pl.ds(8 + r, 8), :] = jnp.where(inside, value, 0.0)
            inside = b > 0 if side == 0 else b < COLS - 1
            value = combine(lambda i: HY[i, side], coefs) + pick(table1 if side == 0 else table0, HBN[side])
            value = jnp.where(inside, value, 0.0)
            for z in range(CZ):
                Z[k, z + 1, pl.ds(7 if side == 0 else 8 + CY, 1), :] = value[z : z + 1, :]
        return total_of(rz), total_of(zs)

    def image(k):
        def plane(z, acc):
            for r in range(0, CY, 8):
                rows, mine = pl.ds(8 + r, 8), pl.ds(r, 8)
                centre = Z[k, z + 1, rows, :]
                value = (
                    CZF[z + 1, mine, :] * Z[k, z + 2, rows, :]
                    + CZF[z, mine, :] * Z[k, z, rows, :]
                    + CYP[z, mine, :] * Z[k, z + 1, pl.ds(9 + r, 8), :]
                    + CYM[z, mine, :] * Z[k, z + 1, pl.ds(7 + r, 8), :]
                    + CXP[z, mine, :] * x_plus(centre)
                    + CXM[z, mine, :] * x_minus(centre)
                )
                value = DG[z, mine, :] * centre - value
                W[k, z, mine, :] = value
                acc = acc + centre * value
            return acc

        return total_of(lax.fori_loop(0, CZ, plane, jnp.zeros((8, NX), f32)))

    def dots_row(values):
        row = jnp.zeros((1, 128), f32)
        for i, value in enumerate(values):
            row = row + jnp.where(lanes_row == 64 + i, value, 0.0)
        return row

    def dot_at(row, i):
        return jnp.sum(jnp.where(lanes_row == 64 + i, row, 0.0), axis=1, keepdims=True)

    for copy in rows_out:
        copy.wait_recv()
    exchange(0, region_sums(R0), jnp.zeros((1, 128), f32))
    lax.fori_loop(0, CY // 8, factor_rows, 0)
    block_solve(R0, BL.at[0])
    halos = send_block_halo(0)

    for copy in bins_out:
        copy.wait_recv()
    low, high = HBZ[0], HBZ[1]
    HBZ[0] = low + jnp.where(low < S_DEV, 84, jnp.where(low < SPAN, 16, jnp.where(low < 36, 32, -32)))
    HBZ[1] = high + jnp.where(high < S_DEV, 88, jnp.where(high < SPAN, 32, jnp.where(high < 36, -16, 32)))
    for z in range(CZ):
        HBN[0, pl.ds(z, 1), :] = HBY[0, z, pl.ds(7, 1), :]
        HBN[1, pl.ds(z, 1), :] = HBY[1, z, pl.ds(0, 1), :] + 92

    tables0, tables1, coefs = [], [], []
    beta1 = gamma = before = power = None
    coefs = []
    for k in range(3):
        t0, t1 = collect(k)
        tables0.append(t0)
        tables1.append(t1)
        if k == 1:
            power, before = dot_at(t1, 0), dot_at(t1, 1)
            alpha0 = before / power
            coefs = [alpha0]
        if k == 2:
            zw, rz, zs = (dot_at(t1, i) for i in range(3))
            beta1 = rz / before
            power, before = zw + 2.0 * beta1 * zs + beta1 * beta1 * power, rz
            alpha1 = before / power
            coefs = [alpha0 + beta1 * alpha1, alpha1]
        for copy in halos:
            copy.wait_recv()
        rz, zs = direction(k, tables0, tables1, coefs, beta1)
        zw = image(k)
        row = dots_row([zw, rz, zs])
        if k < 2:
            exchange(k + 1, region_sums(W.at[k]), row)
            block_solve(W.at[k], BL.at[k + 1])
            halos_next = send_block_halo(k + 1)
            for copy in halos:
                copy.wait_send()
            halos = halos_next
    for copy in halos:
        copy.wait_send()

    M3[...] = row

    def post(n, c):
        ta, tb = partner(n)
        remote(M3, G3.at[me], gs.at[3], gr.at[3], (ta, tb)).start()
        return c

    lax.fori_loop(0, DEVS - 1, post, 0)
    G3[me] = M3[...]
    for copy in halo + bins_out + rows_out:
        copy.wait_send()
    for k in range(3):
        part = M.at[k, pl.ds(0, DEVS - 1)]
        pltpu.make_async_copy(part, part, gs.at[k]).wait()
    part = G3.at[pl.ds(0, DEVS - 1)]
    pltpu.make_async_copy(part, part, gr.at[3]).wait()

    def add(i, acc):
        return acc + G3[pl.ds(8 * i, 8)]

    total = jnp.sum(lax.fori_loop(0, DEVS // 8, add, jnp.zeros((8, 1, 128), f32)), axis=0)
    zw, rz, zs = (dot_at(total, i) for i in range(3))
    beta2 = rz / before
    power = zw + 2.0 * beta2 * zs + beta2 * beta2 * power
    alpha2 = rz / power
    c1 = alpha1 + beta2 * alpha2
    c0 = alpha0 + beta1 * c1

    def finish(z, c):
        for r in range(0, CY, 8):
            rows, inner = pl.ds(r, 8), pl.ds(8 + r, 8)
            out_x[z, rows, :] = c0 * Z[0, z + 1, inner, :] + c1 * Z[1, z + 1, inner, :] + alpha2 * Z[2, z + 1, inner, :]
            out_r[z, rows, :] = R0[z, rows, :] - (
                c0 * W[0, z, rows, :] + c1 * W[1, z, rows, :] + alpha2 * W[2, z, rows, :]
            )
        return c

    lax.fori_loop(0, CZ, finish, 0)
    pltpu.make_async_copy(part, part, gs.at[3]).wait()


def on_device(fraction, source, bubble_label, subdomain, coarse_inverse):
    out = jax.ShapeDtypeStruct(fraction.shape, f32)
    hbm = pl.BlockSpec(memory_space=pl.ANY)
    vmem = pl.BlockSpec(memory_space=pltpu.VMEM)
    block = (CZ, CY, NX)

    def buf(*shape, dtype=f32):
        return pltpu.VMEM(shape, dtype)

    dma = pltpu.SemaphoreType.DMA
    return pl.pallas_call(
        kernel,
        out_shape=(out, out),
        in_specs=[hbm] * 5,
        out_specs=(vmem, vmem),
        scratch_shapes=[
            buf(CZ + 6, 64, NX),
            buf(3, CZ + 4, 64, NX),
            buf(CZ + 2, 64, NX),
            buf(*block),
            buf(*block, dtype=jnp.int32),
            buf(*block, dtype=jnp.int32),
            buf(*block, dtype=jnp.int32),
            buf(SPAN, DEVS * SPAN),
            buf(56, DEVS * SPAN),
            buf(CZ + 1, CY, NX),
            buf(*block),
            buf(*block),
            buf(*block),
            buf(*block),
            buf(*block),
            buf(*block),
            buf(*block),
            buf(3, *block),
            buf(3, *block),
            buf(3, CZ + 2, 48, NX),
            buf(2, CY, NX, dtype=jnp.int32),
            buf(2, CZ, 8, NX, dtype=jnp.int32),
            buf(3, 2, CY, NX),
            buf(3, 2, CZ, NX),
            buf(2, CZ, NX, dtype=jnp.int32),
            buf(3, 2, CZ, NX),
            buf(56, 128),
            buf(48, 256),
            buf(COLS, 48, 128),
            buf(COLS, 48, 128),
            buf(3, DEVS, 2, 128),
            buf(3, DEVS, 2, 128),
            buf(1, 128),
            buf(DEVS, 1, 128),
            dma((5,)),
            dma((8,)),
            dma((8,)),
            dma((4,)),
            dma((4,)),
            dma((2,)),
            dma((2,)),
            dma((3, 4)),
            dma((3, 4)),
            dma((4,)),
            dma((4,)),
        ],
        compiler_params=pltpu.CompilerParams(
            collective_id=0, has_side_effects=True, vmem_limit_bytes=56 * 2**20
        ),
    )(fraction, source, bubble_label, subdomain, coarse_inverse)


def solution(mesh):
    placed = (P("gz", "gy", None),) * 4 + (P(("gz", "gy"), None),)
    return jax.shard_map(
        on_device, mesh=mesh, in_specs=placed, out_specs=(P("gz", "gy", None),) * 2, check_vma=False
    )
```

time: 1010 us -> 144 us (0.14); the launches traced: 993 us -> 144 us
  blocking collectives: 624 us -> 0 us
  Pallas kernels: 0 us -> 140 us
  matrix products: 101 us -> 0 us
  local copies, waits for them, and re-layouts: 95.5 us -> 2.72 us
  starting transfers between devices: 84.6 us -> 0 us
  other arithmetic: 60.3 us -> 0 us
  waiting for transfers between devices: 17.2 us -> 0 us
    psum x8 -> x0, blocking collectives: 624 us -> none  [the longest x3 234 us: precondition(): product = lax.psum(jnp.sum(residual * direction), ('gz', 'gy'))]
    pallas_call x0 -> x1, Pallas kernels: none -> 140 us  [on_device(): pl.pallas_call(kernel, out_shape=(out, out), in_specs=[hbm] * 5, out_spec...]
    dot_general x51 -> x0, matrix products: 101 us -> none  [the longest x24 68.5 us: one_plane(): return jnp.dot(onehot, plane_values, precision=highest)]
    ppermute x30 -> x0, starting transfers between devices: 84.6 us -> none  [the longest x15 56.1 us: with_halo(): lax.ppermute(lax.slice_in_dim(block, block.shape[dim] - width, None, axis...]
    dynamic_slice x48 -> x0, local copies, waits for them, and re-layouts: 52.5 us -> none  [region_sums(): return jnp.sum(lax.map(one_plane, (flat_bins, flat_field)), axis=0)]
    dynamic_update_slice x48 -> x0, local copies, waits for them, and re-layouts: 23.6 us -> none  [the longest x24 23 us: region_values(): return lax.map(one_plane, flat_bins)]
    ppermute x30 -> x0, waiting for transfers between devices: 17.2 us -> none  [the longest x15 9.8 us: with_halo(): lax.ppermute(lax.slice_in_dim(block, block.shape[dim] - width, None, axis...]
    reduce_sum x8 -> x0, other arithmetic: 13.7 us -> none  [the longest x3 9.04 us: on_device(): alpha = product / lax.psum(jnp.sum(search * image), ('gz', 'gy'))]
  transfers between devices with their start and end apart: 30 -> 0, of which waited for: 11 -> 0; matrix products, arithmetic and copies ran while one was open for 2% -> 0% of each run, Pallas kernels for 0% -> 0%
where the time goes in v1:
time: 144 us
  Pallas kernels  140 us (97%)
  local copies, waits for them, and re-layouts  2.72 us (2%)
    pallas_call x1, Pallas kernels, on_device(): pl.pallas_call(kernel, out_shape=(out, out), in_specs=[hbm] * 5, out_spec...  140 us

profile of v1, /device:TPU:1, one launch (start us, length us, event | category | flops | bytes accessed | tf_op | source)
XLA Modules:
  0.0 143.5 jit_solution(16829734230332147945)
XLA Ops:
  0.6 140.2 %shard_map.68 = (f32[8,32,512]{2,1,0:T(8,128)}, f32[8,32,512]{2,1,0:T(8,128)}) custom-call(f32[8,32,512]{2,1,0:T(8,128)} %frac.1, f32[8,32,512]{2,1,0:T(8,128)} %src.1, s32[8,32,512]{2,1,0:T(8,128)} %lab.1, s32[8,32,512]{2,1,0:T(8,128)} %sub.1, f32[20,5120]{1,0:T(8,128)} %cinv.1), custom_call_target="tpu_custom_call" | custom-call | tf_op jit(solution)/shard_map/pallas_call | solution.py:544
  140.8 0.0 copy-start
  140.8 1.9 %copy.9 = f32[8,32,512]{2,1,0:T(8,128)} copy(f32[8,32,512]{2,1,0:T(8,128)} %get-tuple-element.4) | data formatting | bytes 1048576
  142.7 0.0 copy-done
  142.7 0.8 copy.10
Async XLA Ops:
  140.8 1.9 %copy-start = (f32[8,32,512]{2,1,0:T(8,128)S(1)}, f32[8,32,512]{2,1,0:T(8,128)}, u32[]{:S(2)}) copy-start(f32[8,32,512]{2,1,0:T(8,128)} %get-tuple-element.5) | copy-start | bytes 1572868

commit v2 on v1

--- a/solution.py
+++ b/solution.py
@@ -29,21 +29,17 @@
     return jnp.where(lanes_of(v.shape) == 0, 0.0, pltpu.roll(v, 1, 1))
 
 
-def far_first(n, half):
-    return half + ((n + 1) // 2) * (1 - 2 * lax.rem(n, 2))
-
-
 def kernel(
     frac, src, lab, sub, cinv, out_x, out_r,
     F, NRM, KAP, SRC, LB, SB, BN, CV, CW, CZF, CYP, CYM, CXP, CXM, DG, IV,
     R0, W, BL, Z, HBZ, HBY, HZ, HY, HBN, HYO, T2, X, YB, YS, M, G, M3, G3,
-    ld, fs, fr, bsn, brc, cs, cr, ks, kr, gs, gr,
+    ld, fs, fr, bsn, brc, cs, cr, ks, kr, gs, gr, met,
 ):
     a = lax.axis_index("gz")
     b = lax.axis_index("gy")
     me = b * SLABS + a
     here = a * COLS + b
-    phys_y, phys_z, phys_x, core = a // 8, lax.rem(a, 8), b // 2, lax.rem(b, 2)
+    phys_y, phys_z = a // 8, lax.rem(a, 8)
     up, down = lax.rem(a + 1, SLABS), lax.rem(a + SLABS - 1, SLABS)
     right, left = lax.rem(b + 1, COLS), lax.rem(b + COLS - 1, COLS)
 
@@ -58,21 +54,22 @@
         copy.start()
 
     def partner(k):
-        ty = lax.rem(phys_y + far_first(lax.rem(k // 8, 4), 2), 4)
-        tz = lax.rem(phys_z + far_first(k // 32, 4), 8)
-        tx = lax.rem(phys_x + far_first(lax.rem(k // 2, 4), 2), 4)
-        tc = lax.rem(core + 1 - lax.rem(k, 2), 2)
-        ta, tb = ty * 8 + tz, tx * 2 + tc
-        return ta, tb
-
+        t = lax.rem(me + 1 + k, DEVS)
+        return lax.rem(t, SLABS), t // SLABS
+
+    neighbours = [(c, d) for c in (down, a, up) for d in (left, b, right) if c is not a or d is not b]
+    across = [(a, lax.rem(b + k, COLS)) for k in range(1, COLS)]
+    along_z = [(phys_y * 8 + lax.rem(phys_z + k, 8), b) for k in range(1, 8)]
+    along_y = [(lax.rem(phys_y + k, 4) * 8 + phys_z, b) for k in range(1, 4)]
     bar = pltpu.get_barrier_semaphore()
-
-    def greet(k, c):
-        pl.semaphore_signal(bar, inc=1, device_id=partner(k), device_id_type=MESH)
-        return c
-
-    lax.fori_loop(0, DEVS - 1, greet, 0)
-    pl.semaphore_wait(bar, DEVS - 1)
+    first_met = neighbours + across + along_z + along_y
+    for device in first_met:
+        pl.semaphore_signal(bar, inc=1, device_id=device, device_id_type=MESH)
+    pl.semaphore_wait(bar, len(first_met))
+
+    def join(i, group):
+        for device in group:
+            pl.semaphore_signal(met.at[i], inc=1, device_id=device, device_id_type=MESH)
 
     def remote(source, target, send, recv, device):
         return pltpu.make_async_remote_copy(
@@ -91,6 +88,7 @@
     ]
     for copy in halo:
         copy.start()
+    join(0, across)
 
     loads[2].wait()
     loads[3].wait()
@@ -122,6 +120,8 @@
     ]
     for copy in rows_out:
         copy.start()
+    pl.semaphore_wait(met.at[0], len(across))
+    join(1, along_z)
     X[...] = jnp.zeros_like(X)
     YB[...] = jnp.zeros_like(YB)
     YS[...] = jnp.zeros_like(YS)
@@ -131,6 +131,8 @@
     loads[1].wait()
     for copy in halo:
         copy.wait_recv()
+    pl.semaphore_wait(met.at[1], len(along_z))
+    join(2, along_y)
 
     @pl.when(a == 0)
     def _():
@@ -442,9 +444,11 @@
     def dot_at(row, i):
         return jnp.sum(jnp.where(lanes_row == 64 + i, row, 0.0), axis=1, keepdims=True)
 
+    sums = region_sums(R0)
     for copy in rows_out:
         copy.wait_recv()
-    exchange(0, region_sums(R0), jnp.zeros((1, 128), f32))
+    pl.semaphore_wait(met.at[2], len(along_y))
+    exchange(0, sums, jnp.zeros((1, 128), f32))
     lax.fori_loop(0, CY // 8, factor_rows, 0)
     block_solve(R0, BL.at[0])
     halos = send_block_halo(0)
@@ -592,6 +596,7 @@
             dma((3, 4)),
             dma((4,)),
             dma((4,)),
+            pltpu.SemaphoreType.REGULAR((3,)),
         ],
         compiler_params=pltpu.CompilerParams(
             collective_id=0, has_side_effects=True, vmem_limit_bytes=56 * 2**20

time: 144 us -> 95.7 us (0.66)
  Pallas kernels: 140 us -> 92.2 us
    pallas_call x1, Pallas kernels: 140 us -> 92.2 us  [on_device(): pl.pallas_call(kernel, out_shape=(out, out), in_specs=[hbm] * 5, out_spec...]
where the time goes in v2:
time: 95.7 us; the launch traced here: 95.6 us
  Pallas kernels  92.2 us (96%)
  local copies, waits for them, and re-layouts  2.72 us (3%)
    pallas_call x1, Pallas kernels, on_device(): pl.pallas_call(kernel, out_shape=(out, out), in_specs=[hbm] * 5, out_spec...  92.2 us
    unnamed x4, local copies, waits for them, and re-layouts  2.72 us

profile of v2, /device:TPU:1, one launch (start us, length us, event | category | flops | bytes accessed | tf_op | source)
XLA Modules:
  0.0 95.6 jit_solution(15303179491629509379)
XLA Ops:
  0.6 92.2 %shard_map.68 = (f32[8,32,512]{2,1,0:T(8,128)}, f32[8,32,512]{2,1,0:T(8,128)}) custom-call(f32[8,32,512]{2,1,0:T(8,128)} %frac.1, f32[8,32,512]{2,1,0:T(8,128)} %src.1, s32[8,32,512]{2,1,0:T(8,128)} %lab.1, s32[8,32,512]{2,1,0:T(8,128)} %sub.1, f32[20,5120]{1,0:T(8,128)} %cinv.1), custom_call_target="tpu_custom_call" | custom-call | tf_op jit(solution)/shard_map/pallas_call | solution.py:548
  92.8 0.0 copy-start
  92.9 1.9 %copy.9 = f32[8,32,512]{2,1,0:T(8,128)} copy(f32[8,32,512]{2,1,0:T(8,128)} %get-tuple-element.4) | data formatting | bytes 1048576
  94.8 0.0 copy-done
  94.8 0.8 copy.10
Async XLA Ops:
  92.8 1.9 %copy-start = (f32[8,32,512]{2,1,0:T(8,128)S(1)}, f32[8,32,512]{2,1,0:T(8,128)}, u32[]{:S(2)}) copy-start(f32[8,32,512]{2,1,0:T(8,128)} %get-tuple-element.5) | copy-start | bytes 1572868

commit v3 on v2

--- a/solution.py
+++ b/solution.py
@@ -31,7 +31,7 @@
 
 def kernel(
     frac, src, lab, sub, cinv, out_x, out_r,
-    F, NRM, KAP, SRC, LB, SB, BN, CV, CW, CZF, CYP, CYM, CXP, CXM, DG, IV,
+    F, PK, PG, NRM, KAP, SRC, LB, SB, BN, CV, CW, CZF, CYP, CYM, CXP, CXM, DG, IV,
     R0, W, BL, Z, HBZ, HBY, HZ, HY, HBN, HYO, T2, X, YB, YS, M, G, M3, G3,
     ld, fs, fr, bsn, brc, cs, cr, ks, kr, gs, gr, met,
 ):
@@ -53,18 +53,36 @@
     for copy in loads:
         copy.start()
 
-    def partner(k):
-        t = lax.rem(me + 1 + k, DEVS)
-        return lax.rem(t, SLABS), t // SLABS
+    def everyone(post):
+        for away in (4, 3, 5, 2, 6, 1, 7, 0):
+            there = lax.rem(phys_z + away, 8)
+
+            def one(n, c, there=there):
+                t = lax.rem(phys_y * COLS + b + 1 + n, 4 * COLS)
+                post(((t // COLS) * 8 + there, lax.rem(t, COLS)))
+                return c
+
+            lax.fori_loop(0, 4 * COLS - (away == 0), one, 0)
 
     neighbours = [(c, d) for c in (down, a, up) for d in (left, b, right) if c is not a or d is not b]
     across = [(a, lax.rem(b + k, COLS)) for k in range(1, COLS)]
     along_z = [(phys_y * 8 + lax.rem(phys_z + k, 8), b) for k in range(1, 8)]
     along_y = [(lax.rem(phys_y + k, 4) * 8 + phys_z, b) for k in range(1, 4)]
+    corners = (
+        (((10, 47), (10, 46), (9, 47)), ((2, 15), (2, 14), (1, 15))),
+        (((10, 16), (10, 17), (9, 16)), ((2, 48), (2, 49), (1, 48))),
+        (((3, 47), (3, 46), (4, 47)), ((11, 15), (11, 14), (12, 15))),
+        (((3, 16), (3, 17), (4, 16)), ((11, 48), (11, 49), (12, 48))),
+    )
     bar = pltpu.get_barrier_semaphore()
     first_met = neighbours + across + along_z + along_y
     for device in first_met:
         pl.semaphore_signal(bar, inc=1, device_id=device, device_id_type=MESH)
+    loads[0].wait()
+    PK[...] = jnp.zeros_like(PK)
+    for i, (mine, _) in enumerate(corners):
+        for j, (z, y) in enumerate(mine):
+            PK[i, pl.ds(j, 1), :] = F[z, pl.ds(y, 1), :]
     pl.semaphore_wait(bar, len(first_met))
 
     def join(i, group):
@@ -81,10 +99,10 @@
         remote(frac.at[pl.ds(5, 3)], F.at[pl.ds(0, 3), pl.ds(16, CY)], fs.at[1], fr.at[1], (up, b)),
         remote(frac.at[:, pl.ds(24, 8)], F.at[pl.ds(3, CZ), pl.ds(8, 8)], fs.at[2], fr.at[2], (a, right)),
         remote(frac.at[:, pl.ds(0, 8)], F.at[pl.ds(3, CZ), pl.ds(48, 8)], fs.at[3], fr.at[3], (a, left)),
-        remote(frac.at[pl.ds(6, 2), pl.ds(24, 8)], F.at[pl.ds(1, 2), pl.ds(8, 8)], fs.at[4], fr.at[4], (up, right)),
-        remote(frac.at[pl.ds(6, 2), pl.ds(0, 8)], F.at[pl.ds(1, 2), pl.ds(48, 8)], fs.at[5], fr.at[5], (up, left)),
-        remote(frac.at[pl.ds(0, 2), pl.ds(24, 8)], F.at[pl.ds(11, 2), pl.ds(8, 8)], fs.at[6], fr.at[6], (down, right)),
-        remote(frac.at[pl.ds(0, 2), pl.ds(0, 8)], F.at[pl.ds(11, 2), pl.ds(48, 8)], fs.at[7], fr.at[7], (down, left)),
+        remote(PK.at[0], PG.at[0], fs.at[4], fr.at[4], (up, right)),
+        remote(PK.at[1], PG.at[1], fs.at[5], fr.at[5], (up, left)),
+        remote(PK.at[2], PG.at[2], fs.at[6], fr.at[6], (down, right)),
+        remote(PK.at[3], PG.at[3], fs.at[7], fr.at[7], (down, left)),
     ]
     for copy in halo:
         copy.start()
@@ -127,29 +145,6 @@
     YS[...] = jnp.zeros_like(YS)
     T2[...] = jnp.zeros_like(T2)
 
-    loads[0].wait()
-    loads[1].wait()
-    for copy in halo:
-        copy.wait_recv()
-    pl.semaphore_wait(met.at[1], len(along_z))
-    join(2, along_y)
-
-    @pl.when(a == 0)
-    def _():
-        F[pl.ds(0, 3)] = jnp.zeros((3,) + F.shape[1:], f32)
-
-    @pl.when(a == SLABS - 1)
-    def _():
-        F[pl.ds(11, 3)] = jnp.zeros((3,) + F.shape[1:], f32)
-
-    @pl.when(b == 0)
-    def _():
-        F[:, pl.ds(8, 8)] = jnp.zeros((F.shape[0], 8, NX), f32)
-
-    @pl.when(b == COLS - 1)
-    def _():
-        F[:, pl.ds(48, 8)] = jnp.zeros((F.shape[0], 8, NX), f32)
-
     def row_valid(first_row, shape):
         row = lax.broadcasted_iota(jnp.int32, shape, 0) + (first_row - 16 + b * CY)
         return (row >= 0) & (row < COLS * CY)
@@ -175,8 +170,6 @@
             NRM[2, n, rows, :] = gx * scale
         return c
 
-    lax.fori_loop(0, CZ + 4, normals_plane, 0)
-
     def kappa_plane(n, c):
         inside = z_valid(n - 1)
         for r in wide:
@@ -190,8 +183,6 @@
             KAP[n, rows, :] = jnp.where(row_valid(r, value.shape) & inside, value, 0.0)
         return c
 
-    lax.fori_loop(0, CZ + 2, kappa_plane, 0)
-
     def density(v):
         return 1.0 - 0.75 * v
 
@@ -200,8 +191,6 @@
             rows = pl.ds(16 + r, 16)
             CZF[n, pl.ds(r, 16), :] = 2.0 / (density(F[n + 2, rows, :]) + density(F[n + 3, rows, :]))
         return c
-
-    lax.fori_loop(0, CZ + 1, faces_plane, 0)
 
     def assemble_plane(z, c):
         for r in range(0, CY, 8):
@@ -225,7 +214,50 @@
             R0[z, mine, :] = SRC[z, mine, :] - 0.5 * term
         return c
 
-    lax.fori_loop(0, CZ, assemble_plane, 0)
+    loads[1].wait()
+    halo[2].wait_recv()
+    halo[3].wait_recv()
+
+    def clear_rows(first, count):
+        @pl.when(b == 0)
+        def _():
+            F[pl.ds(first, count), pl.ds(8, 8)] = jnp.zeros((count, 8, NX), f32)
+
+        @pl.when(b == COLS - 1)
+        def _():
+            F[pl.ds(first, count), pl.ds(48, 8)] = jnp.zeros((count, 8, NX), f32)
+
+    clear_rows(3, CZ)
+    lax.fori_loop(3, 9, normals_plane, 0)
+    lax.fori_loop(3, 7, kappa_plane, 0)
+    lax.fori_loop(1, CZ, faces_plane, 0)
+    lax.fori_loop(3, 5, assemble_plane, 0)
+
+    for i in (0, 1, 4, 5, 6, 7):
+        halo[i].wait_recv()
+    for i, (_, theirs) in enumerate(corners):
+        for j, (z, y) in enumerate(theirs):
+            F[z, pl.ds(y, 1), :] = PG[i, pl.ds(j, 1), :]
+    pl.semaphore_wait(met.at[1], len(along_z))
+    join(2, along_y)
+    clear_rows(0, 3)
+    clear_rows(11, 3)
+
+    @pl.when(a == 0)
+    def _():
+        F[pl.ds(0, 3)] = jnp.zeros((3,) + F.shape[1:], f32)
+
+    @pl.when(a == SLABS - 1)
+    def _():
+        F[pl.ds(11, 3)] = jnp.zeros((3,) + F.shape[1:], f32)
+
+    def outer(n, count, step):
+        return n + step * (n // count)
+
+    lax.fori_loop(0, 6, lambda n, c: normals_plane(outer(n, 3, 6), c), 0)
+    lax.fori_loop(0, 6, lambda n, c: kappa_plane(outer(n, 3, 4), c), 0)
+    lax.fori_loop(0, 2, lambda n, c: faces_plane(n * CZ, c), 0)
+    lax.fori_loop(0, 6, lambda n, c: assemble_plane(outer(n, 3, 2), c), 0)
 
     def factor_rows(i, c):
         rows = pl.ds(pl.multiple_of(i * 8, 8), 8)
@@ -255,7 +287,7 @@
                     )
                 return tuple(new)
 
-            acc = lax.fori_loop(0, CZ * 4, tile, tuple(jnp.zeros((8, 128), f32) for _ in range(B_DEV)))
+            acc = lax.fori_loop(0, CZ * 4, tile, tuple(jnp.zeros((8, 128), f32) for _ in range(B_DEV)), unroll=4)
             for k in range(B_DEV):
                 T2[pl.ds(8 + B_DEV * group + k, 1), :] = jnp.sum(acc[k], axis=0, keepdims=True)
 
@@ -268,11 +300,11 @@
         for k in range(S_DEV):
             picked = jnp.sum(jnp.where(domain == k, acc, 0.0), axis=0, keepdims=True)
             T2[pl.ds(k, 1), :] = (picked[:, 0:128] + picked[:, 128:256]) + (picked[:, 256:384] + picked[:, 384:512])
-        return jnp.sum(T2[...], axis=1, keepdims=True)
-
-    def exchange(k, sums, dots):
+
+    def exchange(k, count, dots):
+        sums = jnp.sum(T2[pl.ds(0, count), :], axis=1, keepdims=True)
         for g in range(8):
-            part = jnp.sum(CW[:, pl.ds(640 * g, 640)] * sums, axis=0, keepdims=True)
+            part = jnp.sum(CW[pl.ds(0, count), pl.ds(640 * g, 640)] * sums, axis=0, keepdims=True)
             for j in range(4):
                 moved = part if j == 0 else pltpu.roll(part, 640 - 160 * j, 1)
                 X[pl.ds(8 + 4 * g + j, 1), :] = moved[:, 0:256]
@@ -308,12 +340,10 @@
             M[k, pl.ds(SLABS * t, SLABS), 1, :] = row1
             before = row0
 
-        def post(n, c):
-            ta, tb = partner(n)
-            remote(M.at[k, tb * SLABS + ta], G.at[k, me], gs.at[k], gr.at[k], (ta, tb)).start()
-            return c
-
-        lax.fori_loop(0, DEVS - 1, post, 0)
+        def post(device):
+            remote(M.at[k, device[1] * SLABS + device[0]], G.at[k, me], gs.at[k], gr.at[k], device).start()
+
+        everyone(post)
         G[k, me] = M[k, me]
 
     def collect(k):
@@ -444,11 +474,11 @@
     def dot_at(row, i):
         return jnp.sum(jnp.where(lanes_row == 64 + i, row, 0.0), axis=1, keepdims=True)
 
-    sums = region_sums(R0)
+    region_sums(R0)
+    pl.semaphore_wait(met.at[2], len(along_y))
     for copy in rows_out:
         copy.wait_recv()
-    pl.semaphore_wait(met.at[2], len(along_y))
-    exchange(0, sums, jnp.zeros((1, 128), f32))
+    exchange(0, 56, jnp.zeros((1, 128), f32))
     lax.fori_loop(0, CY // 8, factor_rows, 0)
     block_solve(R0, BL.at[0])
     halos = send_block_halo(0)
@@ -485,7 +515,8 @@
         zw = image(k)
         row = dots_row([zw, rz, zs])
         if k < 2:
-            exchange(k + 1, region_sums(W.at[k]), row)
+            region_sums(W.at[k])
+            exchange(k + 1, 56, row)
             block_solve(W.at[k], BL.at[k + 1])
             halos_next = send_block_halo(k + 1)
             for copy in halos:
@@ -496,12 +527,7 @@
 
     M3[...] = row
 
-    def post(n, c):
-        ta, tb = partner(n)
-        remote(M3, G3.at[me], gs.at[3], gr.at[3], (ta, tb)).start()
-        return c
-
-    lax.fori_loop(0, DEVS - 1, post, 0)
+    everyone(lambda device: remote(M3, G3.at[me], gs.at[3], gr.at[3], device).start())
     G3[me] = M3[...]
     for copy in halo + bins_out + rows_out:
         copy.wait_send()
@@ -552,6 +578,8 @@
         out_specs=(vmem, vmem),
         scratch_shapes=[
             buf(CZ + 6, 64, NX),
+            buf(4, 4, NX),
+            buf(4, 4, NX),
             buf(3, CZ + 4, 64, NX),
             buf(CZ + 2, 64, NX),
             buf(*block),

time: 95.7 us -> 89.2 us (0.932)
  Pallas kernels: 92.2 us -> 85.7 us
    pallas_call x1, Pallas kernels: 92.2 us -> 85.7 us  [on_device(): pl.pallas_call(kernel, out_shape=(out, out), in_specs=[hbm] * 5, out_spec...]
where the time goes in v3:
time: 89.2 us; the launch traced here: 89.1 us
  Pallas kernels  85.7 us (96%)
  local copies, waits for them, and re-layouts  2.72 us (3%)
    pallas_call x1, Pallas kernels, on_device(): pl.pallas_call(kernel, out_shape=(out, out), in_specs=[hbm] * 5, out_spec...  85.7 us
    unnamed x4, local copies, waits for them, and re-layouts  2.72 us

profile of v3, /device:TPU:1, one launch (start us, length us, event | category | flops | bytes accessed | tf_op | source)
XLA Modules:
  0.0 89.1 jit_solution(17088351496787420376)
XLA Ops:
  0.6 85.7 %shard_map.68 = (f32[8,32,512]{2,1,0:T(8,128)}, f32[8,32,512]{2,1,0:T(8,128)}) custom-call(f32[8,32,512]{2,1,0:T(8,128)} %frac.1, f32[8,32,512]{2,1,0:T(8,128)} %src.1, s32[8,32,512]{2,1,0:T(8,128)} %lab.1, s32[8,32,512]{2,1,0:T(8,128)} %sub.1, f32[20,5120]{1,0:T(8,128)} %cinv.1), custom_call_target="tpu_custom_call" | custom-call | tf_op jit(solution)/shard_map/pallas_call | solution.py:574
  86.3 0.0 copy-start
  86.4 1.9 %copy.9 = f32[8,32,512]{2,1,0:T(8,128)} copy(f32[8,32,512]{2,1,0:T(8,128)} %get-tuple-element.4) | data formatting | bytes 1048576
  88.3 0.0 copy-done
  88.3 0.8 copy.10
Async XLA Ops:
  86.3 1.9 %copy-start = (f32[8,32,512]{2,1,0:T(8,128)S(1)}, f32[8,32,512]{2,1,0:T(8,128)}, u32[]{:S(2)}) copy-start(f32[8,32,512]{2,1,0:T(8,128)} %get-tuple-element.5) | copy-start | bytes 1572868

commit v4 on v3

--- a/solution.py
+++ b/solution.py
@@ -59,7 +59,7 @@
 
             def one(n, c, there=there):
                 t = lax.rem(phys_y * COLS + b + 1 + n, 4 * COLS)
-                post(((t // COLS) * 8 + there, lax.rem(t, COLS)))
+                post((lax.div(t, COLS) * 8 + there, lax.rem(t, COLS)))
                 return c
 
             lax.fori_loop(0, 4 * COLS - (away == 0), one, 0)
@@ -83,6 +83,26 @@
     for i, (mine, _) in enumerate(corners):
         for j, (z, y) in enumerate(mine):
             PK[i, pl.ds(j, 1), :] = F[z, pl.ds(y, 1), :]
+    loads[2].wait()
+    loads[3].wait()
+
+    def bins_plane(z, c):
+        label, domain = LB[z], SB[z]
+        off = (label >> 7) - a
+        shift = jnp.where(off == 0, S_DEV, jnp.where(off < 0, SPAN, SPAN + B_DEV))
+        BN[z] = jnp.where(label >= 0, (label & 15) + shift, domain - here * S_DEV)
+        return c
+
+    lax.fori_loop(0, CZ, bins_plane, 0)
+    loads[4].wait()
+    first = CV[pl.ds(0, 8), :]
+    CW[pl.ds(0, 8), :] = jnp.where(lax.broadcasted_iota(jnp.int32, first.shape, 0) < S_DEV, first, 0.0)
+    CW[pl.ds(8, B_DEV), :] = CV[pl.ds(S_DEV, B_DEV), :]
+    X[...] = jnp.zeros_like(X)
+    YB[...] = jnp.zeros_like(YB)
+    YS[...] = jnp.zeros_like(YS)
+    T2[...] = jnp.zeros_like(T2)
+
     pl.semaphore_wait(bar, len(first_met))
 
     def join(i, group):
@@ -108,17 +128,6 @@
         copy.start()
     join(0, across)
 
-    loads[2].wait()
-    loads[3].wait()
-
-    def bins_plane(z, c):
-        label, domain = LB[z], SB[z]
-        off = (label >> 7) - a
-        shift = jnp.where(off == 0, S_DEV, jnp.where(off < 0, SPAN, SPAN + B_DEV))
-        BN[z] = jnp.where(label >= 0, (label & 15) + shift, domain - here * S_DEV)
-        return c
-
-    lax.fori_loop(0, CZ, bins_plane, 0)
     bins_out = [
         remote(BN.at[0], HBZ.at[1], bsn.at[0], brc.at[0], (down, b)),
         remote(BN.at[CZ - 1], HBZ.at[0], bsn.at[1], brc.at[1], (up, b)),
@@ -128,10 +137,6 @@
     for copy in bins_out:
         copy.start()
 
-    loads[4].wait()
-    first = CV[pl.ds(0, 8), :]
-    CW[pl.ds(0, 8), :] = jnp.where(lax.broadcasted_iota(jnp.int32, first.shape, 0) < S_DEV, first, 0.0)
-    CW[pl.ds(8, B_DEV), :] = CV[pl.ds(S_DEV, B_DEV), :]
     rows_out = [
         remote(CW.at[pl.ds(8, B_DEV)], CW.at[pl.ds(24, B_DEV)], cs.at[0], cr.at[0], (up, b)),
         remote(CW.at[pl.ds(8, B_DEV)], CW.at[pl.ds(40, B_DEV)], cs.at[1], cr.at[1], (down, b)),
@@ -140,11 +145,6 @@
         copy.start()
     pl.semaphore_wait(met.at[0], len(across))
     join(1, along_z)
-    X[...] = jnp.zeros_like(X)
-    YB[...] = jnp.zeros_like(YB)
-    YS[...] = jnp.zeros_like(YS)
-    T2[...] = jnp.zeros_like(T2)
-
     def row_valid(first_row, shape):
         row = lax.broadcasted_iota(jnp.int32, shape, 0) + (first_row - 16 + b * CY)
         return (row >= 0) & (row < COLS * CY)
@@ -287,7 +287,7 @@
                     )
                 return tuple(new)
 
-            acc = lax.fori_loop(0, CZ * 4, tile, tuple(jnp.zeros((8, 128), f32) for _ in range(B_DEV)), unroll=4)
+            acc = lax.fori_loop(0, CZ * 4, tile, tuple(jnp.zeros((8, 128), f32) for _ in range(B_DEV)), unroll=8)
             for k in range(B_DEV):
                 T2[pl.ds(8 + B_DEV * group + k, 1), :] = jnp.sum(acc[k], axis=0, keepdims=True)
 

time: 89.2 us -> 88 us (0.987)
  Pallas kernels: 85.7 us -> 84.5 us
    pallas_call x1, Pallas kernels: 85.7 us -> 84.5 us  [on_device(): pl.pallas_call(kernel, out_shape=(out, out), in_specs=[hbm] * 5, out_spec...]
where the time goes in v4:
time: 88 us; the launch traced here: 87.9 us
  Pallas kernels  84.5 us (96%)
  local copies, waits for them, and re-layouts  2.72 us (3%)
    pallas_call x1, Pallas kernels, on_device(): pl.pallas_call(kernel, out_shape=(out, out), in_specs=[hbm] * 5, out_spec...  84.5 us
    unnamed x4, local copies, waits for them, and re-layouts  2.72 us

profile of v4, /device:TPU:1, one launch (start us, length us, event | category | flops | bytes accessed | tf_op | source)
XLA Modules:
  0.0 87.9 jit_solution(14054510216669536517)
XLA Ops:
  0.6 84.5 %shard_map.68 = (f32[8,32,512]{2,1,0:T(8,128)}, f32[8,32,512]{2,1,0:T(8,128)}) custom-call(f32[8,32,512]{2,1,0:T(8,128)} %frac.1, f32[8,32,512]{2,1,0:T(8,128)} %src.1, s32[8,32,512]{2,1,0:T(8,128)} %lab.1, s32[8,32,512]{2,1,0:T(8,128)} %sub.1, f32[20,5120]{1,0:T(8,128)} %cinv.1), custom_call_target="tpu_custom_call" | custom-call | tf_op jit(solution)/shard_map/pallas_call | solution.py:574
  85.1 0.0 copy-start
  85.1 1.9 %copy.9 = f32[8,32,512]{2,1,0:T(8,128)} copy(f32[8,32,512]{2,1,0:T(8,128)} %get-tuple-element.4) | data formatting | bytes 1048576
  87.1 0.0 copy-done
  87.1 0.8 copy.10
Async XLA Ops:
  85.1 1.9 %copy-start = (f32[8,32,512]{2,1,0:T(8,128)S(1)}, f32[8,32,512]{2,1,0:T(8,128)}, u32[]{:S(2)}) copy-start(f32[8,32,512]{2,1,0:T(8,128)} %get-tuple-element.5) | copy-start | bytes 1572868
